TPU v7x, 512 devices: a whole 4x8x8 slice. The times are simulated.
512 devices in a mesh: dp: 8 (over y), feat: 64 (over x, z, core).
Axes of the slice: x: 4, y: 8, z: 8, core: 2. Of those that a mesh axis runs over, the one named last changes fastest.
Arguments:
- features: bfloat16 [8, 16384, 128], P('dp', None, 'feat'), may hold values from -6 to 6
- tile_weights: bfloat16 [8, 1536, 128, 128], P('dp', 'feat'), may hold values from -0.15625 to 0.15625
- tile_rows: int32 [8, 1536], P('dp', 'feat'), may hold values from 0 to 1
- tile_owners: int32 [8, 1536, 1], P('dp', 'feat'), may hold values from 0 to 63; in each aligned block of 24 rows (0 to 23, 24 to 47, ..., all dimensions but the last counted through in order) at most 2 rows name the same one
- tile_blocks: int32 [8, 1536], P('dp', 'feat'), may hold values from 0 to 1
- tile_counts: int32 [8, 64], P('dp', 'feat'), may hold values from 6 to 24, as said below
- cotangent: bfloat16 [8, 16384, 1024], P('dp', 'feat'), may hold values from -0.046875 to 0.046875
- w_self: bfloat16 [128, 1024], replicated, may hold values from -0.5 to 0.5
- w_neigh: bfloat16 [128, 1024], replicated, may hold values from -0.5 to 0.5
- bias: float32 [1024], replicated, may hold values from -4 to 4
Outputs:
- grad_self: float32 [128, 1024], P(None, 'feat')
- grad_neigh: float32 [128, 1024], P(None, 'feat')
- grad_bias: float32 [1024], P('feat')
Inputs may be any that keep to these rules, and one draw needn't show every extreme that they name: `tile_owners`: among the 24 tile slots of one device at most 2 name one owner, a bound that some block of them reaches. `tile_counts`: in every batch some device has all 24 slots live.
All inputs are finite; a program needn't handle non-finite values.
Results may differ from a plain program's by a relative error of at most 0.008.
Values may be sent and summed in bfloat16 or wider, within the bound.
No kernel may reach another device: no remote copies, remote signals or barrier semaphores. Data moves between devices by JAX's collectives and lax.ppermute only.
A program may use at most 64 MiB of HBM per device.

v0:
```python
import jax
import jax.numpy as jnp
from jax import lax
from jax.sharding import PartitionSpec as P


def silu_slope(pre_act):
    sigmoid_z = jax.nn.sigmoid(pre_act)
    return sigmoid_z * (1.0 + pre_act * (1.0 - sigmoid_z))


def local(
    features,
    tile_weights,
    tile_rows,
    tile_owners,
    tile_blocks,
    tile_counts,
    cotangent,
    w_self,
    w_neigh,
    bias,
):
    owned = lax.all_to_all(features, "feat", split_axis=1, concat_axis=2, tiled=True)[0]
    node_rows, feat_width = owned.shape
    slot_count = tile_weights.shape[1]
    tile_side = tile_weights.shape[2]
    row_blocks = node_rows // tile_side
    peer_count = lax.axis_size("feat")
    row_index = tile_rows[0]
    owner_index = tile_owners[0, :, 0]
    block_index = tile_blocks[0]
    live = jnp.arange(slot_count, dtype=jnp.int32) < tile_counts[0, 0]
    whole = lax.all_gather(owned, "feat", axis=0, tiled=True)
    picked = whole.reshape(-1, tile_side, feat_width)[owner_index * row_blocks + block_index]
    products = jnp.einsum(
        "kij,kjf->kif", tile_weights[0], picked, preferred_element_type=jnp.float32
    )
    select = (
        (row_index[None, :] == jnp.arange(row_blocks, dtype=jnp.int32)[:, None]) & live[None, :]
    ).astype(jnp.float32)
    summed = jnp.einsum("rk,kif->rif", select, products, precision=lax.Precision.HIGHEST)
    neighbour = summed.reshape(node_rows, feat_width).astype(jnp.bfloat16)
    pre_act = (
        jnp.dot(owned, w_self, preferred_element_type=jnp.float32)
        + jnp.dot(neighbour, w_neigh, preferred_element_type=jnp.float32)
        + bias
    )
    slope = (cotangent[0].astype(jnp.float32) * silu_slope(pre_act)).astype(jnp.bfloat16)
    grad_s = jnp.einsum("nf,nh->fh", owned, slope, preferred_element_type=jnp.float32)
    grad_n = jnp.einsum("nf,nh->fh", neighbour, slope, preferred_element_type=jnp.float32)
    grad_b = jnp.sum(slope.astype(jnp.float32), axis=0)
    total_s, total_n, total_b = lax.psum((grad_s, grad_n, grad_b), ("dp", "feat"))
    column_count = w_self.shape[1] // peer_count
    start = lax.axis_index("feat") * column_count
    out_s = lax.dynamic_slice_in_dim(total_s, start, column_count, 1)
    out_n = lax.dynamic_slice_in_dim(total_n, start, column_count, 1)
    out_b = lax.dynamic_slice_in_dim(total_b, start, column_count, 0)
    return (out_s, out_n, out_b)


def solution(mesh):
    return jax.shard_map(
        local,
        mesh=mesh,
        in_specs=(
            P("dp", None, "feat"),
            P("dp", "feat", None, None),
            P("dp", "feat"),
            P("dp", "feat", None),
            P("dp", "feat"),
            P("dp", "feat"),
            P("dp", "feat", None),
            P(),
            P(),
            P(),
        ),
        out_specs=(P(None, "feat"), P(None, "feat"), P("feat")),
        check_vma=False,
    )
```

profile of v0, /device:TPU:23, one launch (start us, length us, event | category | flops | bytes accessed | tf_op | source)
XLA Modules:
  0.0 554.2 jit_solution(6314317441695136422)
XLA Ops:
  7.2 0.0 copy-start
  7.2 0.0 all-gather.2.cloned.1.call-start
  7.2 15.4 %copy.26 = bf16[1,16384,2]{2,0,1:T(2,128)(2,1)} copy(bf16[1,16384,2]{1,2,0:T(2,128)(2,1)} %param.10) | data formatting | bytes 131072 | tf_op args[0]
  22.6 0.5 broadcast.52
  23.1 90.8 %reduce = bf16[16384,2]{1,0:T(8,128)(2,1)} reduce(bf16[16384,1,2]{2,1,0:T(2,128)(2,1)} %bitcast.51, bf16[]{:T(256)} %broadcast.52), dimensions={1}, to_apply=%bitcast.36.reduce_sub_computation | reduce | bytes 131074
  113.9 7.1 %reshape.61 = bf16[64,2,256]{2,1,0:T(2,128)(2,1)S(1)} reshape(bf16[16384,2]{1,0:T(8,128)(2,1)} %reduce) | data formatting | bytes 131072
  121.0 21.9 %all_to_all.15 = bf16[64,2,256]{2,1,0:T(2,128)(2,1)S(1)} all-to-all(bf16[64,2,256]{2,1,0:T(2,128)(2,1)S(1)} %reshape.61), channel_id=1, replica_groups=mesh['dp'=8,'feat'=64] {'feat'}, dimensions={0} | all-to-all | bytes 131072 | tf_op jit(solution)/shard_map/all_to_all | solution.py:24
  142.9 16.4 %reshape.62 = bf16[16384,1,2]{2,1,0:T(2,128)(2,1)} reshape(bf16[64,2,256]{2,1,0:T(2,128)(2,1)S(1)} %all_to_all.15) | data formatting | bytes 131072
  159.3 0.0 copy-start.5
  159.3 0.0 copy-start.6
  159.3 0.0 copy-start.2
  159.3 15.4 %copy.27 = bf16[1,16384,2]{1,2,0:T(2,128)(2,1)S(1)} copy(bf16[1,16384,2]{2,0,1:T(2,128)(2,1)} %bitcast.52) | data formatting | bytes 131072 | tf_op jit(solution)/shard_map/all_to_all | solution.py:24
  174.7 0.1 copy.28
  174.8 0.7 squeeze.14
  175.4 0.0 all-gather.2.cloned.1.call-update
  175.5 0.2 all-reduce.3.cloned.1.call-start
  176.3 0.0 copy-done.5
  176.4 0.0 copy-done.6
  176.4 0.0 copy-done.2
  176.4 1.2 fusion.10
  177.6 77.5 %all-gather.2.cloned.1.call-done = bf16[16384,128]{0,1:T(8,128)(2,1)} async-done(((bf16[256,128]{0,1:T(8,128)(2,1)}), bf16[16384,128]{0,1:T(8,128)(2,1)}) %all-gather.2.cloned.1.call-update) | async-done | bytes 4194320 | tf_op jit(solution)/shard_map/all_gather | solution.py:34
  255.0 6.4 %copy.29 = bf16[16384,128]{1,0:T(8,128)(2,1)} copy(bf16[16384,128]{0,1:T(8,128)(2,1)} %all-gather.2.cloned.1.call-done) | data formatting | bytes 8388608 | tf_op jit(solution)/shard_map/all_gather | solution.py:34
  261.4 0.0 copy-start.3
  261.4 2.9 gather_fusion
  264.3 0.0 copy-done
  264.4 0.0 copy-start.4
  264.4 1.9 convolution_bitcast_fusion
  266.2 2.0 copy.31
  268.2 0.0 copy-done.3
  268.2 0.6 convolution_convert_fusion
  268.8 0.0 copy-start.1
  268.8 0.0 copy-done.4
  268.9 1.8 convert_reduce_fusion
  270.6 1.1 fusion.11
  271.8 0.0 copy-done.1
  271.8 1.1 convolution_bitcast_fusion.1
  272.9 0.0 all-reduce.3.cloned.1.call-update
  272.9 96.3 %psum.23 = f32[1024]{0:T(1024)S(1)} all-reduce(f32[1024]{0:T(1024)S(1)} %get-tuple-element.5), channel_id=1, replica_groups=mesh['dp'=8,'feat'=64] {'dp','feat'}, use_global_device_ids=true, to_apply=%region_3.0 | all-reduce | flops 1024 | bytes 8192 | tf_op jit(solution)/shard_map/psum | solution.py:53
  369.3 0.6 dynamic_slice.11
  369.9 176.2 %all-reduce.3.cloned.1.call-done = (f32[128,1024]{0,1:T(8,128)}, f32[128,1024]{0,1:T(8,128)}) async-done(((f32[128,1024]{0,1:T(8,128)}, f32[128,1024]{0,1:T(8,128)}), (f32[128,1024]{0,1:T(8,128)}, f32[128,1024]{0,1:T(8,128)})) %all-reduce.3.cloned.1.call-update) | async-done | bytes 1048592 | tf_op jit(solution)/shard_map/psum | solution.py:53
  546.0 1.3 constant_dynamic-slice_fusion
  (5 shorter events, 0.0 us)
Async XLA Ops:
  7.2 257.2 %copy-start = (bf16[1,24,128,128]{3,2,1,0:T(8,128)(2,1)S(1)}, bf16[1,24,128,128]{3,2,1,0:T(8,128)(2,1)}, u32[]{:S(2)}) copy-start(bf16[1,24,128,128]{3,2,1,0:T(8,128)(2,1)} %param.11) | copy-start | bytes 2359300
  7.2 247.8 %all-gather.2.cloned.1.call-start = ((), (), s32[]{:S(2)}) async-start(), calls=%async_computation.1 | async-start | bytes 4259840 | tf_op jit(solution)/shard_map/all_gather | solution.py:34
  159.3 17.1 %copy-start.5 = (s32[1,24]{1,0:T(1,128)S(1)}, s32[1,24]{1,0:T(1,128)}, u32[]{:S(2)}) copy-start(s32[1,24]{1,0:T(1,128)} %param.14) | copy-start | bytes 292
  159.3 17.1 %copy-start.6 = (s32[1,24,1]{1,2,0:T(1,128)S(1)}, s32[1,24,1]{1,2,0:T(1,128)}, u32[]{:S(2)}) copy-start(s32[1,24,1]{1,2,0:T(1,128)} %param.13) | copy-start | bytes 292
  159.3 17.1 %copy-start.2 = (bf16[128,1024]{1,0:T(8,128)(2,1)S(1)}, bf16[128,1024]{1,0:T(8,128)(2,1)}, u32[]{:S(2)}) copy-start(bf16[128,1024]{1,0:T(8,128)(2,1)} %param.17) | copy-start | bytes 786436
  175.5 370.6 %all-reduce.3.cloned.1.call-start = ((), (), s32[]{:S(2)}) async-start(), calls=%async_computation.2 | async-start | bytes 2097152 | tf_op jit(solution)/shard_map/psum | solution.py:53
  261.4 6.8 %copy-start.3 = (s32[1,24]{1,0:T(1,128)S(1)}, s32[1,24]{1,0:T(1,128)}, u32[]{:S(2)}) copy-start(s32[1,24]{1,0:T(1,128)} %param.12) | copy-start | bytes 292
  264.4 4.5 copy-start.4
  268.8 3.0 copy-start.1
Sparse Core Ops, SparseCore 0:
  175.6 79.3 all-gather.1
  273.1 272.9 all-reduce.2
where the time goes:
time: 556 us; the launch traced here: 554 us
  waiting for transfers between devices  254 us (46%)
  blocking collectives  118 us (21%)
  other arithmetic  90.8 us (16%)
  local copies, waits for them, and re-layouts  68.7 us (12%)
  between operations  14.9 us (3%)
  matrix products  7.67 us (1%)
    psum x1, waiting for transfers between devices, local(): lax.psum((grad_s, grad_n, grad_b), ('dp', 'feat'))  176 us
    psum x1, blocking collectives, local(): lax.psum((grad_s, grad_n, grad_b), ('dp', 'feat'))  96.3 us
    unnamed x1, other arithmetic  90.8 us
    all_gather x1, waiting for transfers between devices, local(): whole = lax.all_gather(owned, 'feat', axis=0, tiled=True)  77.5 us
    unnamed x19, local copies, waits for them, and re-layouts  39.5 us
    all_to_all x1, blocking collectives, local(): lax.all_to_all(features, 'feat', split_axis=1, concat_axis=2, tiled=True)[0]  21.9 us
    all_to_all x2, local copies, waits for them, and re-layouts, local(): lax.all_to_all(features, 'feat', split_axis=1, concat_axis=2, tiled=True)[0]  15.5 us
  transfers between devices with their start and end apart: 2, of which 2 were waited for; matrix products, arithmetic and copies ran while one was open for 0% of the time, Pallas kernels for 0%

commit v1 on v0

--- a/solution.py
+++ b/solution.py
@@ -50,7 +50,7 @@
     grad_s = jnp.einsum("nf,nh->fh", owned, slope, preferred_element_type=jnp.float32)
     grad_n = jnp.einsum("nf,nh->fh", neighbour, slope, preferred_element_type=jnp.float32)
     grad_b = jnp.sum(slope.astype(jnp.float32), axis=0)
-    total_s, total_n, total_b = lax.psum((grad_s, grad_n, grad_b), ("dp", "feat"))
+    total_s, total_n, total_b = lax.psum(lax.psum((grad_s, grad_n, grad_b), "dp"), "feat")
     column_count = w_self.shape[1] // peer_count
     start = lax.axis_index("feat") * column_count
     out_s = lax.dynamic_slice_in_dim(total_s, start, column_count, 1)

time: 556 us -> 562 us (1.011)
  the two profiles are of different devices: /device:TPU:23 before, /device:TPU:8 now
where the time goes in v1:
time: 562 us; the launch traced here: 561 us
  waiting for transfers between devices  216 us (38%)
  blocking collectives  163 us (29%)
  other arithmetic  90.8 us (16%)
  local copies, waits for them, and re-layouts  68.9 us (12%)
  between operations  14.6 us (3%)
  matrix products  7.7 us (1%)
    psum x1, blocking collectives, local(): lax.psum(lax.psum((grad_s, grad_n, grad_b), 'dp'), 'feat')  125 us
    unnamed x1, other arithmetic  90.7 us
    psum x1, waiting for transfers between devices, local(): lax.psum((grad_s, grad_n, grad_b), 'dp')  79.9 us
    all_gather x1, waiting for transfers between devices, local(): whole = lax.all_gather(owned, 'feat', axis=0, tiled=True)  75.8 us
    psum x1, waiting for transfers between devices, local(): lax.psum(lax.psum((grad_s, grad_n, grad_b), 'dp'), 'feat')  60.1 us
    unnamed x19, local copies, waits for them, and re-layouts  39.6 us
    all_to_all x1, blocking collectives, local(): lax.all_to_all(features, 'feat', split_axis=1, concat_axis=2, tiled=True)[0]  23.3 us
    all_to_all x2, local copies, waits for them, and re-layouts, local(): lax.all_to_all(features, 'feat', split_axis=1, concat_axis=2, tiled=True)[0]  15.5 us
  transfers between devices with their start and end apart: 3, of which 3 were waited for; matrix products, arithmetic and copies ran while one was open for 0% of the time, Pallas kernels for 0%

profile of v1, /device:TPU:8, one launch (start us, length us, event | category | flops | bytes accessed | tf_op | source)
XLA Modules:
  0.0 561.0 jit_solution(4517570862706635124)
XLA Ops:
  7.2 0.0 copy-start
  7.2 0.0 all-gather.2.cloned.1.call-start
  7.2 15.4 %copy.26 = bf16[1,16384,2]{2,0,1:T(2,128)(2,1)} copy(bf16[1,16384,2]{1,2,0:T(2,128)(2,1)} %param.10) | data formatting | bytes 131072 | tf_op args[0]
  22.6 0.5 broadcast.52
  23.1 90.7 %reduce = bf16[16384,2]{1,0:T(8,128)(2,1)} reduce(bf16[16384,1,2]{2,1,0:T(2,128)(2,1)} %bitcast.51, bf16[]{:T(256)} %broadcast.52), dimensions={1}, to_apply=%bitcast.36.reduce_sub_computation | reduce | bytes 131074
  113.9 7.1 %reshape.61 = bf16[64,2,256]{2,1,0:T(2,128)(2,1)S(1)} reshape(bf16[16384,2]{1,0:T(8,128)(2,1)} %reduce) | data formatting | bytes 131072
  121.0 23.3 %all_to_all.15 = bf16[64,2,256]{2,1,0:T(2,128)(2,1)S(1)} all-to-all(bf16[64,2,256]{2,1,0:T(2,128)(2,1)S(1)} %reshape.61), channel_id=1, replica_groups=mesh['dp'=8,'feat'=64] {'feat'}, dimensions={0} | all-to-all | bytes 131072 | tf_op jit(solution)/shard_map/all_to_all | solution.py:24
  144.3 16.5 %reshape.62 = bf16[16384,1,2]{2,1,0:T(2,128)(2,1)} reshape(bf16[64,2,256]{2,1,0:T(2,128)(2,1)S(1)} %all_to_all.15) | data formatting | bytes 131072
  160.8 0.0 copy-start.5
  160.8 0.0 copy-start.6
  160.8 0.0 copy-start.2
  160.8 15.4 %copy.27 = bf16[1,16384,2]{1,2,0:T(2,128)(2,1)S(1)} copy(bf16[1,16384,2]{2,0,1:T(2,128)(2,1)} %bitcast.52) | data formatting | bytes 131072 | tf_op jit(solution)/shard_map/all_to_all | solution.py:24
  176.3 0.1 copy.28
  176.3 0.7 squeeze.14
  177.0 0.0 all-gather.2.cloned.1.call-update
  177.0 0.2 all-reduce.7.cloned.1.call-start
  177.9 0.0 copy-done.5
  177.9 0.0 copy-done.6
  178.0 0.0 copy-done.2
  178.0 1.2 fusion.10
  179.1 75.8 %all-gather.2.cloned.1.call-done = bf16[16384,128]{0,1:T(8,128)(2,1)} async-done(((bf16[256,128]{0,1:T(8,128)(2,1)}), bf16[16384,128]{0,1:T(8,128)(2,1)}) %all-gather.2.cloned.1.call-update) | async-done | bytes 4194320 | tf_op jit(solution)/shard_map/all_gather | solution.py:34
  254.9 6.4 %copy.29 = bf16[16384,128]{1,0:T(8,128)(2,1)} copy(bf16[16384,128]{0,1:T(8,128)(2,1)} %all-gather.2.cloned.1.call-done) | data formatting | bytes 8388608 | tf_op jit(solution)/shard_map/all_gather | solution.py:34
  261.3 0.0 copy-start.3
  261.4 2.9 gather_fusion
  264.3 0.0 copy-done
  264.3 0.0 copy-start.4
  264.3 1.9 convolution_bitcast_fusion
  266.1 2.0 copy.31
  268.1 0.0 copy-done.3
  268.1 0.6 convolution_convert_fusion
  268.7 0.0 copy-start.1
  268.8 0.0 copy-done.4
  268.8 1.8 convert_reduce_fusion
  270.5 1.2 fusion.11
  271.7 0.0 copy-done.1
  271.7 1.1 convolution_bitcast_fusion.1
  272.9 0.0 all-reduce.7.cloned.1.call-update
  272.9 0.0 all-reduce.5.cloned.1.call-start
  272.9 79.9 %all-reduce.7.cloned.1.call-done = (f32[128,1024]{0,1:T(8,128)}, f32[128,1024]{0,1:T(8,128)}) async-done(((f32[128,1024]{0,1:T(8,128)}, f32[128,1024]{0,1:T(8,128)}), (f32[128,1024]{0,1:T(8,128)}, f32[128,1024]{0,1:T(8,128)})) %all-reduce.7.cloned.1.call-update) | async-done | bytes 1048592 | tf_op jit(solution)/shard_map/psum | solution.py:53
  352.8 0.0 all-reduce.5.cloned.1.call-update
  352.8 14.9 %psum.46 = f32[1024]{0:T(1024)S(1)} all-reduce(f32[1024]{0:T(1024)S(1)} %get-tuple-element.7), channel_id=1, replica_groups=mesh['dp'=8,'feat'=64] {'dp'}, use_global_device_ids=true, to_apply=%region_5.0 | all-reduce | flops 1024 | bytes 8192 | tf_op jit(solution)/shard_map/psum | solution.py:53
  367.7 124.8 %psum.47 = f32[1024]{0:T(1024)S(1)} all-reduce(f32[1024]{0:T(1024)S(1)} %psum.46), channel_id=1, replica_groups=mesh['dp'=8,'feat'=64] {'feat'}, use_global_device_ids=true, to_apply=%region_6.0 | all-reduce | flops 1024 | bytes 8192 | tf_op jit(solution)/shard_map/psum | solution.py:53
  492.4 0.6 dynamic_slice.11
  493.0 60.1 %all-reduce.5.cloned.1.call-done = (f32[128,1024]{0,1:T(8,128)}, f32[128,1024]{0,1:T(8,128)}) async-done(((f32[128,1024]{0,1:T(8,128)}, f32[128,1024]{0,1:T(8,128)}), (f32[128,1024]{0,1:T(8,128)}, f32[128,1024]{0,1:T(8,128)})) %all-reduce.5.cloned.1.call-update) | async-done | bytes 1048592 | tf_op jit(solution)/shard_map/psum | solution.py:53
  553.1 1.3 constant_dynamic-slice_fusion
  (5 shorter events, 0.0 us)
Async XLA Ops:
  7.2 257.1 %copy-start = (bf16[1,24,128,128]{3,2,1,0:T(8,128)(2,1)S(1)}, bf16[1,24,128,128]{3,2,1,0:T(8,128)(2,1)}, u32[]{:S(2)}) copy-start(bf16[1,24,128,128]{3,2,1,0:T(8,128)(2,1)} %param.11) | copy-start | bytes 2359300
  7.2 247.8 %all-gather.2.cloned.1.call-start = ((), (), s32[]{:S(2)}) async-start(), calls=%async_computation.1 | async-start | bytes 4259840 | tf_op jit(solution)/shard_map/all_gather | solution.py:34
  160.8 17.1 %copy-start.5 = (s32[1,24]{1,0:T(1,128)S(1)}, s32[1,24]{1,0:T(1,128)}, u32[]{:S(2)}) copy-start(s32[1,24]{1,0:T(1,128)} %param.14) | copy-start | bytes 292
  160.8 17.1 %copy-start.6 = (s32[1,24,1]{1,2,0:T(1,128)S(1)}, s32[1,24,1]{1,2,0:T(1,128)}, u32[]{:S(2)}) copy-start(s32[1,24,1]{1,2,0:T(1,128)} %param.13) | copy-start | bytes 292
  160.8 17.1 %copy-start.2 = (bf16[128,1024]{1,0:T(8,128)(2,1)S(1)}, bf16[128,1024]{1,0:T(8,128)(2,1)}, u32[]{:S(2)}) copy-start(bf16[128,1024]{1,0:T(8,128)(2,1)} %param.17) | copy-start | bytes 786436
  177.0 175.8 %all-reduce.7.cloned.1.call-start = ((), (), s32[]{:S(2)}) async-start(), calls=%async_computation.3 | async-start | bytes 2097152 | tf_op jit(solution)/shard_map/psum | solution.py:53
  261.3 6.8 %copy-start.3 = (s32[1,24]{1,0:T(1,128)S(1)}, s32[1,24]{1,0:T(1,128)}, u32[]{:S(2)}) copy-start(s32[1,24]{1,0:T(1,128)} %param.12) | copy-start | bytes 292
  264.3 4.5 copy-start.4
  268.7 3.0 copy-start.1
  272.9 280.3 %all-reduce.5.cloned.1.call-start = ((), (), s32[]{:S(2)}) async-start(), calls=%async_computation.2 | async-start | bytes 2097152 | tf_op jit(solution)/shard_map/psum | solution.py:53
Sparse Core Ops, SparseCore 0:
  177.2 77.7 all-gather.1
  273.0 79.7 all-reduce.6
  356.3 196.8 all-reduce.4
